TPU v7x, 32 devices: a whole 2x2x4 slice. The times are simulated.
32 devices in a mesh: groups: 2 (over y), tensor: 4 (over z), vocab: 2 (over x), seq: 2 (over core).
Axes of the slice: x: 2, y: 2, z: 4, core: 2. Of those that a mesh axis runs over, the one named last changes fastest.
Arguments:
- heads_out: bfloat16 [4, 32, 1024], P(('groups', 'seq'), None, 'tensor'), parts along dimension 0, may hold values from -6 to 6
- out_weight: bfloat16 [1024, 5120], P('tensor', 'vocab'), may hold values from -0.1875 to 0.1875
- residual: bfloat16 [4, 32, 5120], P(('groups', 'seq'), 'tensor', 'vocab'), parts along dimension 0, may hold values from -32 to 32
- norm_gain: bfloat16 [5120], P('vocab'), may hold values from 0.5 to 1.5
- head_weight: bfloat16 [6144, 5120], P(('tensor', 'vocab', 'seq')), may hold values from -8 to 8
- targets: int32 [4, 32], P('groups'), parts along dimension 0, may hold values from 0 to 6143
- lengths: int32 [2], P('groups'), parts along dimension 0, may hold values from 16 to 64
Outputs:
- logprobs: float32 [4, 32], P(('groups', 'seq'), 'tensor'), parts along dimension 0
- entropies: float32 [4, 32], P(('groups', 'seq'), 'tensor'), parts along dimension 0
There are 2 independent parts, one for each index of `groups`. A program takes and returns all parts, laid end to end along the dimension named above; an argument that names none is the same for every part. Nothing has to cross between parts.
All inputs are finite; a program needn't handle non-finite values.
Results may differ from a plain program's by a relative error of at most 0.0061.
Values may be sent and summed in bfloat16 or wider, within the bound.
A program may use at most 64 MiB of HBM per device.

v0:
```python
import jax
import jax.numpy as jnp
from jax import lax
from jax.sharding import PartitionSpec as P

D = 5120


norm_epsilon = 1e-05


def on_device(heads_out, out_weight, residual, norm_gain, head_weight, targets, lengths):
    span_rows = heads_out.shape[1]
    shard_rows = residual.shape[1]
    tensor_index = lax.axis_index("tensor")
    seq_index = lax.axis_index("seq")
    tensor_count = lax.axis_size("tensor")
    seq_count = lax.axis_size("seq")
    gain = norm_gain.astype(jnp.float32)
    local_rows = heads_out[0]
    own_rows = residual[0].astype(jnp.float32)
    summed = lax.psum_scatter(
        jnp.dot(local_rows, out_weight, preferred_element_type=jnp.float32),
        "tensor",
        scatter_dimension=0,
        tiled=True,
    )
    hidden = summed + own_rows
    local_squares = jnp.sum(hidden * hidden, axis=1)
    squares = lax.psum(local_squares, "vocab")
    normed = (hidden * lax.rsqrt(squares / D + norm_epsilon)[:, None] * gain).astype(jnp.bfloat16)
    full_rows = lax.all_gather(normed[None], "vocab", axis=2, tiled=True)
    logits = jnp.einsum(
        "gtd,vd->gtv",
        lax.all_gather(full_rows, ("tensor", "seq"), axis=0, tiled=True),
        head_weight,
        preferred_element_type=jnp.float32,
    )
    ordered = targets.reshape(seq_count, tensor_count, shard_rows).transpose(1, 0, 2)
    ordered = ordered.reshape(tensor_count * seq_count, shard_rows)
    own_group = tensor_index * seq_count + seq_index
    vocab_start = lax.axis_index(("tensor", "vocab", "seq")) * head_weight.shape[0]
    local_target = ordered - vocab_start
    columns = lax.broadcasted_iota(jnp.int32, logits.shape, 2)
    chosen = jnp.sum(jnp.where(columns == local_target[..., None], logits, 0.0), axis=2)
    top_local = jnp.max(logits, axis=2)
    top = lax.pmax(top_local, ("tensor", "vocab", "seq"))
    shifted = logits - top[..., None]
    weights = jnp.exp(shifted)
    total, moment, chosen = lax.psum(
        (jnp.sum(weights, axis=2), jnp.sum(weights * shifted, axis=2), chosen),
        ("tensor", "vocab", "seq"),
    )
    log_total = jnp.log(total)
    logprob = chosen - top - log_total
    entropy = log_total - moment / total
    logprob = lax.dynamic_index_in_dim(logprob, own_group, 0, keepdims=False)
    entropy = lax.dynamic_index_in_dim(entropy, own_group, 0, keepdims=False)
    positions = (
        seq_index * span_rows + tensor_index * shard_rows + jnp.arange(shard_rows, dtype=jnp.int32)
    )
    live = positions < lengths[0]
    logprob = jnp.where(live, logprob, 0.0)
    entropy = jnp.where(live, entropy, 0.0)
    return (logprob[None], entropy[None])


def solution(mesh):
    in_specs = (
        P(("groups", "seq"), None, "tensor"),
        P("tensor", "vocab"),
        P(("groups", "seq"), "tensor", "vocab"),
        P("vocab"),
        P(("tensor", "vocab", "seq"), None),
        P("groups", None),
        P("groups"),
    )
    out_specs = (P(("groups", "seq"), "tensor"), P(("groups", "seq"), "tensor"))
    return jax.shard_map(
        on_device, mesh=mesh, in_specs=in_specs, out_specs=out_specs, check_vma=False
    )
```

profile of v0, /device:TPU:0, one launch (start us, length us, event | category | flops | bytes accessed | tf_op | source)
XLA Modules:
  0.0 160.1 jit_solution(10560182976348937178)
XLA Ops:
  7.2 0.0 copy-start
  7.2 0.0 reduce-scatter.2.cloned.1.call-start
  7.2 1.3 copy-done
  8.5 1.8 %fusion.4 = f32[32,2560]{1,0:T(8,128)} fusion(bf16[256,2560]{1,0:T(8,128)(2,1)S(1)} %copy-done, bf16[1,32,256]{2,1,0:T(8,128)(2,1)} %param.7), kind=kOutput, calls=%fused_computation.11 | convolution fusion | flops 41943040 | bytes 1654784 | tf_op jit(solution)/shard_map/dot_general | solution.py:23
  10.2 0.0 reduce-scatter.2.cloned.1.call-update
  10.3 0.7 convert_element_type.14
  11.0 0.7 broadcast_subtract_fusion
  11.7 0.1 sub.38
  12.4 20.8 %reduce-scatter.2.cloned.1.call-done = f32[8,2560]{1,0:T(8,128)} async-done(((f32[32,2560]{1,0:T(8,128)}), f32[8,2560]{1,0:T(8,128)}) %reduce-scatter.2.cloned.1.call-update) | async-done | bytes 81936 | tf_op jit(solution)/shard_map/reduce_scatter | solution.py:22
  33.2 1.0 multiply_reduce_fusion
  34.2 4.9 %psum.28 = f32[8]{0:T(128)S(1)} all-reduce(f32[8]{0:T(128)S(1)} %multiply_reduce_fusion), channel_id=1, replica_groups=mesh['groups'=2,'tensor'=4,'vocab'=2,'seq'=2] {'vocab'}, use_global_device_ids=true, to_apply=%region_2.0 | all-reduce | flops 8 | bytes 64 | tf_op jit(solution)/shard_map/psum | solution.py:30
  39.1 1.0 multiply_convert_fusion
  40.1 4.7 %all-gather = bf16[8,5120]{1,0:T(8,128)(2,1)S(1)} all-gather(bf16[8,2560]{1,0:T(8,128)(2,1)S(1)} %multiply_convert_fusion), channel_id=2, replica_groups=mesh['groups'=2,'tensor'=4,'vocab'=2,'seq'=2] {'vocab'}, dimensions={1}, use_global_device_ids=true | all-gather | bytes 122880 | tf_op jit(solution)/shard_map/all_gather | solution.py:32
  44.8 15.4 %all-gather.1 = bf16[64,5120]{1,0:T(8,128)(2,1)S(1)} all-gather(bf16[8,5120]{1,0:T(8,128)(2,1)S(1)} %all-gather), channel_id=3, replica_groups=mesh['groups'=2,'tensor'=4,'vocab'=2,'seq'=2] {'tensor','seq'}, dimensions={0}, use_global_device_ids=true | all-gather | bytes 737280 | tf_op jit(solution)/shard_map/all_gather | solution.py:35
  60.2 3.5 %fusion.6 = (f32[8,8]{1,0:T(8,128)S(1)}, f32[8,8,384]{2,1,0:T(8,128)S(1)}) fusion(bf16[384,5120]{1,0:T(8,128)(2,1)} %param.11, bf16[64,5120]{1,0:T(8,128)(2,1)S(1)} %all-gather.1), kind=kOutput, calls=%fused_computation.20 | convolution fusion | flops 251682752 | bytes 4686080 | tf_op jit(solution)/shard_map/gtd,vd->gtv/dot_general | solution.py:33
  63.7 31.2 %pmax.7 = f32[8,8]{1,0:T(8,128)S(1)} all-reduce(f32[8,8]{1,0:T(8,128)S(1)} %get-tuple-element.10), channel_id=1, replica_groups=mesh['groups'=2,'tensor'=4,'vocab'=2,'seq'=2] {'tensor','vocab','seq'}, use_global_device_ids=true, to_apply=%region_6.7 | all-reduce | flops 64 | bytes 512 | tf_op jit(solution)/shard_map/pmax | solution.py:47
  94.9 0.2 fusion.3
  95.1 57.6 %all-reduce = (f32[8,8]{1,0:T(8,128)S(1)}, f32[8,8]{1,0:T(8,128)S(1)}, f32[8,8]{1,0:T(8,128)S(1)}) all-reduce(f32[8,8]{1,0:T(8,128)S(1)} %get-tuple-element.4, f32[8,8]{1,0:T(8,128)S(1)} %get-tuple-element.3, f32[8,8]{1,0:T(8,128)S(1)} %get-tuple-element.2), channel_id=1, replica_groups=mesh['groups'=2,'tensor'=4,'vocab'=2,'seq'=2] {'tensor','vocab','seq'}, use_global_device_ids=true, to_apply=%region_4.5 | all-reduce | flops 192 | bytes 1536 | tf_op jit(solution)/shard_map/psum | solution.py:50
  152.7 0.5 compare_select_fusion
  (3 shorter events, 0.0 us)
Async XLA Ops:
  7.2 1.3 copy-start
  7.2 26.0 %reduce-scatter.2.cloned.1.call-start = ((), (), s32[]{:S(2)}) async-start(), calls=%async_computation.1 | async-start | bytes 409600 | tf_op jit(solution)/shard_map/reduce_scatter | solution.py:22
Sparse Core Ops, SparseCore 0:
  10.4 22.7 reduce-scatter.1
where the time goes:
time: 161 us; the launch traced here: 160 us
  blocking collectives  114 us (71%)
  waiting for transfers between devices  20.8 us (13%)
  between operations  14.7 us (9%)
  matrix products  5.26 us (3%)
  other arithmetic  4.1 us (3%)
    psum x1, blocking collectives, on_device(): lax.psum((jnp.sum(weights, axis=2), jnp.sum(weights * shifted, axis=2), c...  57.6 us
    pmax x1, blocking collectives, on_device(): top = lax.pmax(top_local, ('tensor', 'vocab', 'seq'))  31.2 us
    reduce_scatter x1, waiting for transfers between devices, on_device(): lax.psum_scatter(jnp.dot(local_rows, out_weight, preferred_element_type=j...  20.8 us
    all_gather x1, blocking collectives, on_device(): lax.all_gather(full_rows, ('tensor', 'seq'), axis=0, tiled=True)  15.4 us
    psum x1, blocking collectives, on_device(): squares = lax.psum(local_squares, 'vocab')  4.94 us
    all_gather x1, blocking collectives, on_device(): full_rows = lax.all_gather(normed[None], 'vocab', axis=2, tiled=True)  4.68 us
    dot_general x1, matrix products, on_device(): jnp.einsum('gtd,vd->gtv', lax.all_gather(full_rows, ('tensor', 'seq'), ax...  3.5 us
  transfers between devices with their start and end apart: 1, of which 1 were waited for; matrix products, arithmetic and copies ran while one was open for 1% of the time, Pallas kernels for 0%

commit v1 on v0

v1 whole, which is shorter than its diff:
```python
import jax
import jax.numpy as jnp
from jax import lax
from jax.experimental import pallas as pl
from jax.experimental.pallas import tpu as pltpu
from jax.sharding import PartitionSpec as P

norm_epsilon = 1e-05
MESH = pl.DeviceIdType.MESH
TENSOR, VOCAB, SEQ = 4, 2, 2
PEERS = [
    (dt, dv, ds) for dt in range(TENSOR) for dv in range(VOCAB) for ds in range(SEQ)
][1:]


def fused_kernel(
    heads_ref, weight_hbm, residual_ref, gain_ref, head_hbm, targets_ref, lengths_ref,
    logprob_ref, entropy_ref,
    weight, head, part, part_in, square_out, square_in, rows, stat_out, stat_in,
    weight_sem, head_sem, part_send, part_recv, square_send, square_recv,
    z_send, z_recv, x_send, x_recv, near_send, near_recv, far_send, far_recv,
    stat_send, stat_recv,
):
    t = lax.axis_index("tensor")
    v = lax.axis_index("vocab")
    s = lax.axis_index("seq")
    g = lax.axis_index("groups")
    depth = weight.shape[1]
    half = depth // 2
    shard = part.shape[1]
    span = TENSOR * shard
    width = VOCAB * depth

    def device(dt, dv, ds):
        return (g, lax.rem(t + dt, TENSOR), lax.rem(v + dv, VOCAB), lax.rem(s + ds, SEQ))

    def block(k):
        return lax.rem(t + TENSOR - k, TENSOR)

    def send(src, dst, send_sem, recv_sem, to):
        copy = pltpu.make_async_remote_copy(
            src_ref=src, dst_ref=dst, send_sem=send_sem, recv_sem=recv_sem,
            device_id=to, device_id_type=MESH,
        )
        copy.start()
        return copy

    weight_copy = pltpu.make_async_copy(weight_hbm, weight, weight_sem)
    weight_copy.start()
    head_copy = pltpu.make_async_copy(head_hbm, head, head_sem)
    head_copy.start()
    barrier = pltpu.get_barrier_semaphore()
    for peer in PEERS:
        pl.semaphore_signal(barrier, inc=1, device_id=device(*peer), device_id_type=MESH)

    weight_copy.wait()
    product = jnp.dot(heads_ref[0], weight[...], preferred_element_type=jnp.float32)
    part[...] = product.reshape(TENSOR, shard, depth)
    pl.semaphore_wait(barrier, len(PEERS))
    sent = []
    part_copies = [
        send(part.at[lax.rem(t + k, TENSOR)], part_in.at[k - 1],
             part_send.at[k - 1], part_recv.at[k - 1], device(k, 0, 0))
        for k in range(1, TENSOR)
    ]
    hidden = part[t] + residual_ref[0].astype(jnp.float32)
    for k in range(1, TENSOR):
        part_copies[k - 1].wait_recv()
        hidden = hidden + part_in[k - 1]
    sent += part_copies

    own_square = jnp.sum(hidden * hidden, axis=1, keepdims=True)
    square_out[...] = jnp.broadcast_to(own_square, square_out.shape)
    square_copy = send(square_out, square_in, square_send, square_recv, device(0, 1, 0))
    scaled_gain = gain_ref[...].astype(jnp.float32)
    square_copy.wait_recv()
    sent.append(square_copy)
    mean = (own_square + square_in[:, :1]) / width
    normed = hidden * lax.rsqrt(mean + norm_epsilon) * scaled_gain
    rows[0, 0, t] = jnp.concatenate([normed[:, :half], normed[:, half:]], axis=0).astype(
        jnp.bfloat16
    )

    own = rows.at[0, 0, t]
    z_copies = [
        send(own, own, z_send.at[k - 1], z_recv.at[k - 1], device(k, 0, 0))
        for k in range(1, TENSOR)
    ]
    x_copies, near_copies, far_copies = [], [], []
    for k in range(TENSOR):
        if k:
            z_copies[k - 1].wait_recv()
        here = rows.at[0, 0, block(k)]
        x_copies.append(
            send(here, rows.at[1, 0, block(k)], x_send.at[k], x_recv.at[k], device(0, 1, 0))
        )
        near_copies.append(
            send(here, rows.at[0, 1, block(k)], near_send.at[k], near_recv.at[k],
                 device(0, 0, 1))
        )
    for copy in near_copies:
        copy.wait_recv()
    head_copy.wait()

    blocks = SEQ * TENSOR
    vocab = head.shape[0]

    def partial_logits(side, column_half):
        columns = lax.rem(v + side, VOCAB) * depth + column_half * half
        tokens = rows[side].reshape(blocks * 2 * shard, half)
        out = lax.dot_general(
            tokens, head[:, pl.ds(pl.multiple_of(columns, 128), half)],
            (((1,), (1,)), ((), ())), preferred_element_type=jnp.float32,
        )
        return out.reshape(blocks, 2, shard, vocab)[:, column_half]

    logits = partial_logits(0, 0)
    for k in range(TENSOR):
        x_copies[k].wait_recv()
        far_copies.append(
            send(rows.at[1, 0, block(k)], rows.at[1, 1, block(k)], far_send.at[k],
                 far_recv.at[k], device(0, 0, 1))
        )
    logits = logits + partial_logits(0, 1)
    for copy in far_copies:
        copy.wait_recv()
    logits = logits + partial_logits(1, 0) + partial_logits(1, 1)
    logits = logits.reshape(blocks * shard, vocab)
    sent += z_copies + x_copies + near_copies + far_copies

    diagonal = lax.broadcasted_iota(jnp.int32, (span, span), 0) == lax.broadcasted_iota(
        jnp.int32, (span, span), 1
    )
    all_targets = targets_ref[...].astype(jnp.float32)
    lower, upper = all_targets[0:1], all_targets[1:2]
    own_targets = jnp.where(s == 0, lower, upper)
    other_targets = jnp.where(s == 0, upper, lower)
    target = jnp.concatenate(
        [
            jnp.sum(jnp.where(diagonal, line, 0.0), axis=1, keepdims=True)
            for line in (own_targets, other_targets)
        ],
        axis=0,
    ).astype(jnp.int32)
    start = ((t * VOCAB + v) * SEQ + s) * vocab
    columns = lax.broadcasted_iota(jnp.int32, logits.shape, 1)
    chosen = jnp.sum(
        jnp.where(columns == target - start, logits, 0.0), axis=1, keepdims=True
    )
    top = jnp.max(logits, axis=1, keepdims=True)
    shifted = logits - top
    weights = jnp.exp(shifted)
    total = jnp.sum(weights, axis=1, keepdims=True)
    moment = jnp.sum(weights * shifted, axis=1, keepdims=True)
    lane = lax.broadcasted_iota(jnp.int32, (blocks * shard, 128), 1)
    stats = jnp.where(
        lane == 0, top, jnp.where(lane == 1, total, jnp.where(lane == 2, moment, chosen))
    )
    stat_out[...] = stats.reshape(SEQ, TENSOR, shard, 128)
    stat_in[0] = stat_out[0, t]
    stat_copies = []
    for index, (dt, dv, ds) in enumerate(PEERS):
        stat_copies.append(
            send(stat_out.at[ds, lax.rem(t + dt, TENSOR)], stat_in.at[index + 1],
                 stat_send.at[index], stat_recv.at[index], device(dt, dv, ds))
        )
    for copy in stat_copies:
        copy.wait_recv()
    sent += stat_copies

    gathered = stat_in[...]
    tops = gathered[:, :, 0:1]
    top = jnp.max(tops, axis=0)
    below = tops - top[None]
    scale = jnp.exp(below)
    totals = gathered[:, :, 1:2]
    total = jnp.sum(totals * scale, axis=0)
    moment = jnp.sum(scale * (gathered[:, :, 2:3] + totals * below), axis=0)
    chosen = jnp.sum(gathered[:, :, 3:4], axis=0)
    log_total = jnp.log(total)
    logprob = chosen - top - log_total
    entropy = log_total - moment / total
    shape = (shard, shard)
    diagonal = lax.broadcasted_iota(jnp.int32, shape, 0) == lax.broadcasted_iota(
        jnp.int32, shape, 1
    )
    position = s * span + t * shard + lax.broadcasted_iota(jnp.int32, (1, shard), 1)
    live = position < lengths_ref[0]
    for ref, column in ((logprob_ref, logprob), (entropy_ref, entropy)):
        line = jnp.sum(jnp.where(diagonal, column, 0.0), axis=0, keepdims=True)
        ref[...] = jnp.where(live, line, 0.0)
    for copy in sent:
        copy.wait_send()


def fused(heads_out, out_weight, residual, norm_gain, head_weight, targets, lengths):
    shard = residual.shape[1]
    features, depth = out_weight.shape
    vocab, width = head_weight.shape
    vmem = pl.BlockSpec(memory_space=pltpu.VMEM)
    hbm = pl.BlockSpec(memory_space=pl.ANY)
    dma = pltpu.SemaphoreType.DMA
    f32, bf16 = jnp.float32, jnp.bfloat16
    hops = TENSOR - 1
    return pl.pallas_call(
        fused_kernel,
        out_shape=(jax.ShapeDtypeStruct((1, shard), f32),) * 2,
        in_specs=[vmem, hbm, vmem, vmem, hbm, vmem, pl.BlockSpec(memory_space=pltpu.SMEM)],
        out_specs=(vmem, vmem),
        scratch_shapes=[
            pltpu.VMEM((features, depth), bf16),
            pltpu.VMEM((vocab, width), bf16),
            pltpu.VMEM((TENSOR, shard, depth), f32),
            pltpu.VMEM((hops, shard, depth), f32),
            pltpu.VMEM((shard, 128), f32),
            pltpu.VMEM((shard, 128), f32),
            pltpu.VMEM((VOCAB, SEQ, TENSOR, 2 * shard, depth // 2), bf16),
            pltpu.VMEM((SEQ, TENSOR, shard, 128), f32),
            pltpu.VMEM((len(PEERS) + 1, shard, 128), f32),
            dma, dma, dma((hops,)), dma((hops,)), dma, dma,
            dma((hops,)), dma((hops,)), dma((TENSOR,)), dma((TENSOR,)),
            dma((TENSOR,)), dma((TENSOR,)), dma((TENSOR,)), dma((TENSOR,)),
            dma((len(PEERS),)), dma((len(PEERS),)),
        ],
        compiler_params=pltpu.CompilerParams(
            collective_id=0, has_side_effects=True, vmem_limit_bytes=32 * 1024 * 1024
        ),
    )(
        heads_out, out_weight, residual, norm_gain.reshape(1, depth), head_weight,
        targets, lengths,
    )


def general(heads_out, out_weight, residual, norm_gain, head_weight, targets, lengths):
    span_rows = heads_out.shape[1]
    shard_rows = residual.shape[1]
    tensor_index = lax.axis_index("tensor")
    seq_index = lax.axis_index("seq")
    tensor_count = lax.axis_size("tensor")
    seq_count = lax.axis_size("seq")
    gain = norm_gain.astype(jnp.float32)
    summed = lax.psum_scatter(
        jnp.dot(heads_out[0], out_weight, preferred_element_type=jnp.float32),
        "tensor", scatter_dimension=0, tiled=True,
    )
    hidden = summed + residual[0].astype(jnp.float32)
    squares = lax.psum(jnp.sum(hidden * hidden, axis=1), "vocab")
    width = head_weight.shape[1]
    normed = (hidden * lax.rsqrt(squares / width + norm_epsilon)[:, None] * gain).astype(
        jnp.bfloat16
    )
    full_rows = lax.all_gather(normed[None], "vocab", axis=2, tiled=True)
    logits = jnp.einsum(
        "gtd,vd->gtv",
        lax.all_gather(full_rows, ("tensor", "seq"), axis=0, tiled=True),
        head_weight,
        preferred_element_type=jnp.float32,
    )
    ordered = targets.reshape(seq_count, tensor_count, shard_rows).transpose(1, 0, 2)
    ordered = ordered.reshape(tensor_count * seq_count, shard_rows)
    own_group = tensor_index * seq_count + seq_index
    axes = ("tensor", "vocab", "seq")
    local_target = ordered - lax.axis_index(axes) * head_weight.shape[0]
    columns = lax.broadcasted_iota(jnp.int32, logits.shape, 2)
    chosen = jnp.sum(jnp.where(columns == local_target[..., None], logits, 0.0), axis=2)
    top = lax.pmax(jnp.max(logits, axis=2), axes)
    shifted = logits - top[..., None]
    weights = jnp.exp(shifted)
    total, moment, chosen = lax.psum(
        (jnp.sum(weights, axis=2), jnp.sum(weights * shifted, axis=2), chosen), axes
    )
    log_total = jnp.log(total)
    logprob = chosen - top - log_total
    entropy = log_total - moment / total
    logprob = lax.dynamic_index_in_dim(logprob, own_group, 0, keepdims=False)
    entropy = lax.dynamic_index_in_dim(entropy, own_group, 0, keepdims=False)
    positions = (
        seq_index * span_rows + tensor_index * shard_rows + jnp.arange(shard_rows, dtype=jnp.int32)
    )
    live = positions < lengths[0]
    return (jnp.where(live, logprob, 0.0)[None], jnp.where(live, entropy, 0.0)[None])


def solution(mesh):
    in_specs = (
        P(("groups", "seq"), None, "tensor"),
        P("tensor", "vocab"),
        P(("groups", "seq"), "tensor", "vocab"),
        P("vocab"),
        P(("tensor", "vocab", "seq"), None),
        P("groups", None),
        P("groups"),
    )
    out_specs = (P(("groups", "seq"), "tensor"), P(("groups", "seq"), "tensor"))
    sizes = (mesh.shape["tensor"], mesh.shape["vocab"], mesh.shape["seq"])
    body = fused if sizes == (TENSOR, VOCAB, SEQ) else general
    return jax.shard_map(
        body, mesh=mesh, in_specs=in_specs, out_specs=out_specs, check_vma=False
    )
```

time: 161 us -> 40.7 us (0.25)
  blocking collectives: 114 us -> 0 us
  Pallas kernels: 0 us -> 31.7 us
  waiting for transfers between devices: 20.8 us -> 0 us
  between operations: 14.7 us -> 1.29 us
  local copies, waits for them, and re-layouts: 1.36 us -> 7.32 us
  matrix products: 5.26 us -> 0 us
  other arithmetic: 4.1 us -> 0 us
    psum x2 -> x0, blocking collectives: 62.6 us -> none  [the longest x1 57.6 us: on_device(): lax.psum((jnp.sum(weights, axis=2), jnp.sum(weights * shifted, axis=2), c...]
    pallas_call x0 -> x1, Pallas kernels: none -> 31.7 us  [fused(): pl.pallas_call(fused_kernel, out_shape=(jax.ShapeDtypeStruct((1, shard),...]
    pmax x1 -> x0, blocking collectives: 31.2 us -> none  [on_device(): top = lax.pmax(top_local, ('tensor', 'vocab', 'seq'))]
    reduce_scatter x1 -> x0, waiting for transfers between devices: 20.8 us -> none  [on_device(): lax.psum_scatter(jnp.dot(local_rows, out_weight, preferred_element_type=j...]
    all_gather x2 -> x0, blocking collectives: 20.1 us -> none  [the longest x1 15.4 us: on_device(): lax.all_gather(full_rows, ('tensor', 'seq'), axis=0, tiled=True)]
    unnamed x2 -> x12, local copies, waits for them, and re-layouts: 1.27 us -> 6.62 us
    dot_general x2 -> x0, matrix products: 5.26 us -> none  [the longest x1 3.5 us: on_device(): jnp.einsum('gtd,vd->gtv', lax.all_gather(full_rows, ('tensor', 'seq'), ax...]
    convert_element_type x2 -> x0, other arithmetic: 1.67 us -> none  [the longest x1 0.97 us: on_device(): (hidden * lax.rsqrt(squares / D + norm_epsilon)[:, None] * gain).astype(j...]
  transfers between devices with their start and end apart: 1 -> 0, of which waited for: 1 -> 0; matrix products, arithmetic and copies ran while one was open for 1% -> 0% of each run, Pallas kernels for 0% -> 0%
where the time goes in v1:
time: 40.7 us; the launch traced here: 40.4 us
  Pallas kernels  31.7 us (78%)
  local copies, waits for them, and re-layouts  7.32 us (18%)
  between operations  1.29 us (3%)
    pallas_call x1, Pallas kernels, fused(): pl.pallas_call(fused_kernel, out_shape=(jax.ShapeDtypeStruct((1, shard),...  31.7 us
    unnamed x12, local copies, waits for them, and re-layouts  6.62 us

profile of v1, /device:TPU:0, one launch (start us, length us, event | category | flops | bytes accessed | tf_op | source)
XLA Modules:
  0.0 40.4 jit_solution(9564088773958211495)
XLA Ops:
  1.3 0.7 %reshape.7.gain_ref = bf16[1,2560]{1,0:T(2,128)(2,1)S(1)} reshape(bf16[2560]{0:T(1024)(128)(2,1)} %param.10) | data formatting | bytes 10240 | tf_op jit(solution)/shard_map/reshape | solution.py:229
  2.0 0.0 copy-start
  2.0 2.1 %copy-done = bf16[384,5120]{1,0:T(8,128)(2,1)S(1)} copy-done((bf16[384,5120]{1,0:T(8,128)(2,1)S(1)}, bf16[384,5120]{1,0:T(8,128)(2,1)}, u32[]{:S(2)}) %copy-start) | copy-done | bytes 3932184
  4.1 0.0 copy-start.1
  4.1 1.3 %copy-done.1 = bf16[256,2560]{1,0:T(8,128)(2,1)S(1)} copy-done((bf16[256,2560]{1,0:T(8,128)(2,1)S(1)}, bf16[256,2560]{1,0:T(8,128)(2,1)}, u32[]{:S(2)}) %copy-start.1) | copy-done | bytes 1310744
  5.4 0.0 copy-start.2
  5.4 0.8 %copy-done.2 = bf16[1,8,2560]{2,1,0:T(8,128)(2,1)S(1)} copy-done((bf16[1,8,2560]{2,1,0:T(8,128)(2,1)S(1)}, bf16[1,8,2560]{2,1,0:T(8,128)(2,1)}, u32[]{:S(2)}) %copy-start.2) | copy-done | bytes 40984
  6.2 0.0 copy-start.3
  6.2 0.7 %copy-done.3 = bf16[1,32,256]{2,1,0:T(8,128)(2,1)S(1)} copy-done((bf16[1,32,256]{2,1,0:T(8,128)(2,1)S(1)}, bf16[1,32,256]{2,1,0:T(8,128)(2,1)}, u32[]{:S(2)}) %copy-start.3) | copy-done | bytes 16408
  6.9 0.0 copy-start.4
  6.9 0.7 %copy-done.4 = s32[2,32]{1,0:T(2,128)S(1)} copy-done((s32[2,32]{1,0:T(2,128)S(1)}, s32[2,32]{1,0:T(2,128)}, u32[]{:S(2)}) %copy-start.4) | copy-done | bytes 280
  7.6 31.7 %shard_map.86 = (f32[1,8]{1,0:T(1,128)S(1)}, f32[1,8]{1,0:T(1,128)S(1)}) custom-call(bf16[1,32,256]{2,1,0:T(8,128)(2,1)S(1)} %copy-done.3, bf16[256,2560]{1,0:T(8,128)(2,1)S(1)} %copy-done.1, bf16[1,8,2560]{2,1,0:T(8,128)(2,1)S(1)} %copy-done.2, bf16[1,2560]{1,0:T(2,128)(2,1)S(1)} %reshape.7.gain_ref, bf16[384,5120]{1,0:T(8,128)(2,1)S(1)} %copy-done, ...), custom_call_target="tpu_custom_call" | custom-call | tf_op jit(solution)/shard_map/pallas_call | solution.py:205
  39.3 0.5 %copy.12 = f32[1,8]{1,0:T(1,128)} copy(f32[1,8]{1,0:T(1,128)S(1)} %get-tuple-element.4) | data formatting | bytes 64
  39.9 0.5 %copy.13 = f32[1,8]{1,0:T(1,128)} copy(f32[1,8]{1,0:T(1,128)S(1)} %get-tuple-element.5) | data formatting | bytes 64
Async XLA Ops:
  2.0 2.1 %copy-start = (bf16[384,5120]{1,0:T(8,128)(2,1)S(1)}, bf16[384,5120]{1,0:T(8,128)(2,1)}, u32[]{:S(2)}) copy-start(bf16[384,5120]{1,0:T(8,128)(2,1)} %head_hbm.1) | copy-start | bytes 11796484
  4.1 1.3 %copy-start.1 = (bf16[256,2560]{1,0:T(8,128)(2,1)S(1)}, bf16[256,2560]{1,0:T(8,128)(2,1)}, u32[]{:S(2)}) copy-start(bf16[256,2560]{1,0:T(8,128)(2,1)} %weight_hbm.1) | copy-start | bytes 3932164
  5.4 0.8 %copy-start.2 = (bf16[1,8,2560]{2,1,0:T(8,128)(2,1)S(1)}, bf16[1,8,2560]{2,1,0:T(8,128)(2,1)}, u32[]{:S(2)}) copy-start(bf16[1,8,2560]{2,1,0:T(8,128)(2,1)} %residual_ref.1) | copy-start | bytes 122884
  6.2 0.7 %copy-start.3 = (bf16[1,32,256]{2,1,0:T(8,128)(2,1)S(1)}, bf16[1,32,256]{2,1,0:T(8,128)(2,1)}, u32[]{:S(2)}) copy-start(bf16[1,32,256]{2,1,0:T(8,128)(2,1)} %heads_ref.1) | copy-start | bytes 49156
  6.9 0.7 %copy-start.4 = (s32[2,32]{1,0:T(2,128)S(1)}, s32[2,32]{1,0:T(2,128)}, u32[]{:S(2)}) copy-start(s32[2,32]{1,0:T(2,128)} %targets_ref.1) | copy-start | bytes 772

commit v2 on v1

--- a/solution.py
+++ b/solution.py
@@ -14,10 +14,10 @@
 
 
 def fused_kernel(
-    heads_ref, weight_hbm, residual_ref, gain_ref, head_hbm, targets_ref, lengths_ref,
+    heads_hbm, weight_hbm, residual_hbm, gain_ref, head_hbm, targets_hbm, lengths_hbm,
     logprob_ref, entropy_ref,
-    weight, head, part, part_in, square_out, square_in, rows, stat_out, stat_in,
-    weight_sem, head_sem, part_send, part_recv, square_send, square_recv,
+    heads_ref, residual_ref, targets_ref, lengths_ref, weight, head, part, part_in, square_out, square_in, rows, stat_out, stat_in,
+    input_sem, weight_sem, head_sem, part_send, part_recv, square_send, square_recv,
     z_send, z_recv, x_send, x_recv, near_send, near_recv, far_send, far_recv,
     stat_send, stat_recv,
 ):
@@ -45,15 +45,24 @@
         copy.start()
         return copy
 
+    heads_copy = pltpu.make_async_copy(heads_hbm, heads_ref, input_sem.at[0])
+    heads_copy.start()
     weight_copy = pltpu.make_async_copy(weight_hbm, weight, weight_sem)
     weight_copy.start()
+    residual_copy = pltpu.make_async_copy(residual_hbm, residual_ref, input_sem.at[1])
+    residual_copy.start()
+    targets_copy = pltpu.make_async_copy(targets_hbm, targets_ref, input_sem.at[2])
+    targets_copy.start()
+    lengths_copy = pltpu.make_async_copy(lengths_hbm, lengths_ref, input_sem.at[3])
+    lengths_copy.start()
     head_copy = pltpu.make_async_copy(head_hbm, head, head_sem)
-    head_copy.start()
     barrier = pltpu.get_barrier_semaphore()
     for peer in PEERS:
         pl.semaphore_signal(barrier, inc=1, device_id=device(*peer), device_id_type=MESH)
 
+    heads_copy.wait()
     weight_copy.wait()
+    head_copy.start()
     product = jnp.dot(heads_ref[0], weight[...], preferred_element_type=jnp.float32)
     part[...] = product.reshape(TENSOR, shard, depth)
     pl.semaphore_wait(barrier, len(PEERS))
@@ -63,6 +72,7 @@
              part_send.at[k - 1], part_recv.at[k - 1], device(k, 0, 0))
         for k in range(1, TENSOR)
     ]
+    residual_copy.wait()
     hidden = part[t] + residual_ref[0].astype(jnp.float32)
     for k in range(1, TENSOR):
         part_copies[k - 1].wait_recv()
@@ -72,7 +82,7 @@
     own_square = jnp.sum(hidden * hidden, axis=1, keepdims=True)
     square_out[...] = jnp.broadcast_to(own_square, square_out.shape)
     square_copy = send(square_out, square_in, square_send, square_recv, device(0, 1, 0))
-    scaled_gain = gain_ref[...].astype(jnp.float32)
+    scaled_gain = gain_ref[...].astype(jnp.float32).reshape(1, depth)
     square_copy.wait_recv()
     sent.append(square_copy)
     mean = (own_square + square_in[:, :1]) / width
@@ -98,6 +108,12 @@
             send(here, rows.at[0, 1, block(k)], near_send.at[k], near_recv.at[k],
                  device(0, 0, 1))
         )
+    for k in range(TENSOR):
+        x_copies[k].wait_recv()
+        far_copies.append(
+            send(rows.at[1, 0, block(k)], rows.at[1, 1, block(k)], far_send.at[k],
+                 far_recv.at[k], device(0, 0, 1))
+        )
     for copy in near_copies:
         copy.wait_recv()
     head_copy.wait()
@@ -115,12 +131,6 @@
         return out.reshape(blocks, 2, shard, vocab)[:, column_half]
 
     logits = partial_logits(0, 0)
-    for k in range(TENSOR):
-        x_copies[k].wait_recv()
-        far_copies.append(
-            send(rows.at[1, 0, block(k)], rows.at[1, 1, block(k)], far_send.at[k],
-                 far_recv.at[k], device(0, 0, 1))
-        )
     logits = logits + partial_logits(0, 1)
     for copy in far_copies:
         copy.wait_recv()
@@ -131,6 +141,7 @@
     diagonal = lax.broadcasted_iota(jnp.int32, (span, span), 0) == lax.broadcasted_iota(
         jnp.int32, (span, span), 1
     )
+    targets_copy.wait()
     all_targets = targets_ref[...].astype(jnp.float32)
     lower, upper = all_targets[0:1], all_targets[1:2]
     own_targets = jnp.where(s == 0, lower, upper)
@@ -184,6 +195,7 @@
     diagonal = lax.broadcasted_iota(jnp.int32, shape, 0) == lax.broadcasted_iota(
         jnp.int32, shape, 1
     )
+    lengths_copy.wait()
     position = s * span + t * shard + lax.broadcasted_iota(jnp.int32, (1, shard), 1)
     live = position < lengths_ref[0]
     for ref, column in ((logprob_ref, logprob), (entropy_ref, entropy)):
@@ -205,9 +217,13 @@
     return pl.pallas_call(
         fused_kernel,
         out_shape=(jax.ShapeDtypeStruct((1, shard), f32),) * 2,
-        in_specs=[vmem, hbm, vmem, vmem, hbm, vmem, pl.BlockSpec(memory_space=pltpu.SMEM)],
+        in_specs=[hbm, hbm, hbm, vmem, hbm, hbm, hbm],
         out_specs=(vmem, vmem),
         scratch_shapes=[
+            pltpu.VMEM(heads_out.shape, bf16),
+            pltpu.VMEM(residual.shape, bf16),
+            pltpu.VMEM(targets.shape, jnp.int32),
+            pltpu.SMEM(lengths.shape, jnp.int32),
             pltpu.VMEM((features, depth), bf16),
             pltpu.VMEM((vocab, width), bf16),
             pltpu.VMEM((TENSOR, shard, depth), f32),
@@ -217,16 +233,16 @@
             pltpu.VMEM((VOCAB, SEQ, TENSOR, 2 * shard, depth // 2), bf16),
             pltpu.VMEM((SEQ, TENSOR, shard, 128), f32),
             pltpu.VMEM((len(PEERS) + 1, shard, 128), f32),
-            dma, dma, dma((hops,)), dma((hops,)), dma, dma,
+            dma((4,)), dma, dma, dma((hops,)), dma((hops,)), dma, dma,
             dma((hops,)), dma((hops,)), dma((TENSOR,)), dma((TENSOR,)),
             dma((TENSOR,)), dma((TENSOR,)), dma((TENSOR,)), dma((TENSOR,)),
             dma((len(PEERS),)), dma((len(PEERS),)),
         ],
         compiler_params=pltpu.CompilerParams(
-            collective_id=0, has_side_effects=True, vmem_limit_bytes=32 * 1024 * 1024
+            collective_id=0, has_side_effects=True, vmem_limit_bytes=60 * 1024 * 1024
         ),
     )(
-        heads_out, out_weight, residual, norm_gain.reshape(1, depth), head_weight,
+        heads_out, out_weight, residual, norm_gain, head_weight,
         targets, lengths,
     )
 

time: 40.7 us -> 36.9 us (0.907)
  local copies, waits for them, and re-layouts: 7.32 us -> 2.25 us
  Pallas kernels: 31.7 us -> 33 us
    unnamed x12 -> x2, local copies, waits for them, and re-layouts: 6.62 us -> 2.25 us
    pallas_call x1, Pallas kernels: 31.7 us -> 33 us  [fused(): pl.pallas_call(fused_kernel, out_shape=(jax.ShapeDtypeStruct((1, shard),...]
    reshape x1 -> x0, local copies, waits for them, and re-layouts: 0.7 us -> none  [fused(): norm_gain.reshape(1, depth)]
where the time goes in v2:
time: 36.9 us; the launch traced here: 36.6 us
  Pallas kernels  33 us (89%)
  local copies, waits for them, and re-layouts  2.25 us (6%)
  between operations  1.29 us (3%)
    pallas_call x1, Pallas kernels, fused(): pl.pallas_call(fused_kernel, out_shape=(jax.ShapeDtypeStruct((1, shard),...  33 us
    unnamed x2, local copies, waits for them, and re-layouts  2.25 us

profile of v2, /device:TPU:0, one launch (start us, length us, event | category | flops | bytes accessed | tf_op | source)
XLA Modules:
  0.0 36.6 jit_solution(658870453833814809)
XLA Ops:
  1.3 33.0 %shard_map.86 = (f32[1,8]{1,0:T(1,128)}, f32[1,8]{1,0:T(1,128)}) custom-call(bf16[1,32,256]{2,1,0:T(8,128)(2,1)} %heads_hbm.1, bf16[256,2560]{1,0:T(8,128)(2,1)} %weight_hbm.1, bf16[1,8,2560]{2,1,0:T(8,128)(2,1)} %residual_hbm.1, bf16[2560]{0:T(1024)(128)(2,1)} %gain_ref.1, bf16[384,5120]{1,0:T(8,128)(2,1)} %head_hbm.1, s32[2,32]{1,0:T(2,128)} %targets_hbm.1, ...), custom_call_target="tpu_custom_call" | custom-call | tf_op jit(solution)/shard_map/pallas_call | solution.py:217
  34.3 1.1 %copy.12 = f32[1,8]{1,0:T(1,128)} copy(f32[1,8]{1,0:T(1,128)} %get-tuple-element.4) | data formatting | bytes 64
  35.4 1.1 %copy.13 = f32[1,8]{1,0:T(1,128)} copy(f32[1,8]{1,0:T(1,128)} %get-tuple-element.5) | data formatting | bytes 64

commit v3 on v2

--- a/solution.py
+++ b/solution.py
@@ -15,7 +15,7 @@
 
 def fused_kernel(
     heads_hbm, weight_hbm, residual_hbm, gain_ref, head_hbm, targets_hbm, lengths_hbm,
-    logprob_ref, entropy_ref,
+    out_ref,
     heads_ref, residual_ref, targets_ref, lengths_ref, weight, head, part, part_in, square_out, square_in, rows, stat_out, stat_in,
     input_sem, weight_sem, head_sem, part_send, part_recv, square_send, square_recv,
     z_send, z_recv, x_send, x_recv, near_send, near_recv, far_send, far_recv,
@@ -96,7 +96,7 @@
         send(own, own, z_send.at[k - 1], z_recv.at[k - 1], device(k, 0, 0))
         for k in range(1, TENSOR)
     ]
-    x_copies, near_copies, far_copies = [], [], []
+    x_copies = []
     for k in range(TENSOR):
         if k:
             z_copies[k - 1].wait_recv()
@@ -104,16 +104,10 @@
         x_copies.append(
             send(here, rows.at[1, 0, block(k)], x_send.at[k], x_recv.at[k], device(0, 1, 0))
         )
-        near_copies.append(
-            send(here, rows.at[0, 1, block(k)], near_send.at[k], near_recv.at[k],
-                 device(0, 0, 1))
-        )
+    near_copies = [send(rows.at[0, 0], rows.at[0, 1], near_send, near_recv, device(0, 0, 1))]
     for k in range(TENSOR):
         x_copies[k].wait_recv()
-        far_copies.append(
-            send(rows.at[1, 0, block(k)], rows.at[1, 1, block(k)], far_send.at[k],
-                 far_recv.at[k], device(0, 0, 1))
-        )
+    far_copies = [send(rows.at[1, 0], rows.at[1, 1], far_send, far_recv, device(0, 0, 1))]
     for copy in near_copies:
         copy.wait_recv()
     head_copy.wait()
@@ -198,9 +192,9 @@
     lengths_copy.wait()
     position = s * span + t * shard + lax.broadcasted_iota(jnp.int32, (1, shard), 1)
     live = position < lengths_ref[0]
-    for ref, column in ((logprob_ref, logprob), (entropy_ref, entropy)):
+    for index, column in enumerate((logprob, entropy)):
         line = jnp.sum(jnp.where(diagonal, column, 0.0), axis=0, keepdims=True)
-        ref[...] = jnp.where(live, line, 0.0)
+        out_ref[index] = jnp.where(live, line, 0.0)
     for copy in sent:
         copy.wait_send()
 
@@ -214,11 +208,11 @@
     dma = pltpu.SemaphoreType.DMA
     f32, bf16 = jnp.float32, jnp.bfloat16
     hops = TENSOR - 1
-    return pl.pallas_call(
+    both = pl.pallas_call(
         fused_kernel,
-        out_shape=(jax.ShapeDtypeStruct((1, shard), f32),) * 2,
+        out_shape=jax.ShapeDtypeStruct((2, 1, shard), f32),
         in_specs=[hbm, hbm, hbm, vmem, hbm, hbm, hbm],
-        out_specs=(vmem, vmem),
+        out_specs=vmem,
         scratch_shapes=[
             pltpu.VMEM(heads_out.shape, bf16),
             pltpu.VMEM(residual.shape, bf16),
@@ -235,7 +229,7 @@
             pltpu.VMEM((len(PEERS) + 1, shard, 128), f32),
             dma((4,)), dma, dma, dma((hops,)), dma((hops,)), dma, dma,
             dma((hops,)), dma((hops,)), dma((TENSOR,)), dma((TENSOR,)),
-            dma((TENSOR,)), dma((TENSOR,)), dma((TENSOR,)), dma((TENSOR,)),
+            dma, dma, dma, dma,
             dma((len(PEERS),)), dma((len(PEERS),)),
         ],
         compiler_params=pltpu.CompilerParams(
@@ -245,6 +239,7 @@
         heads_out, out_weight, residual, norm_gain, head_weight,
         targets, lengths,
     )
+    return (both[0], both[1])
 
 
 def general(heads_out, out_weight, residual, norm_gain, head_weight, targets, lengths):

time: 36.9 us -> 35.7 us (0.967)
  local copies, waits for them, and re-layouts: 2.25 us -> 1.18 us
    unnamed x2 -> x0, local copies, waits for them, and re-layouts: 2.25 us -> none
    squeeze x0 -> x1, local copies, waits for them, and re-layouts: none -> 1.18 us  [fused(): return (both[0], both[1])]
where the time goes in v3:
time: 35.7 us; the launch traced here: 35.4 us
  Pallas kernels  32.9 us (92%)
  between operations  1.29 us (4%)
  local copies, waits for them, and re-layouts  1.18 us (3%)
    pallas_call x1, Pallas kernels, fused(): pl.pallas_call(fused_kernel, out_shape=jax.ShapeDtypeStruct((2, 1, shard)...  32.9 us
    squeeze x1, local copies, waits for them, and re-layouts, fused(): return (both[0], both[1])  1.18 us

profile of v3, /device:TPU:0, one launch (start us, length us, event | category | flops | bytes accessed | tf_op | source)
XLA Modules:
  0.0 35.4 jit_solution(10731060035251214392)
XLA Ops:
  1.3 32.9 %shard_map.86 = f32[2,1,8]{2,1,0:T(1,128)} custom-call(bf16[1,32,256]{2,1,0:T(8,128)(2,1)} %heads_hbm.1, bf16[256,2560]{1,0:T(8,128)(2,1)} %weight_hbm.1, bf16[1,8,2560]{2,1,0:T(8,128)(2,1)} %residual_hbm.1, bf16[2560]{0:T(1024)(128)(2,1)} %gain_ref.1, bf16[384,5120]{1,0:T(8,128)(2,1)} %head_hbm.1, s32[2,32]{1,0:T(2,128)} %targets_hbm.1, s32[1]{0:T(128)S(6)} %copy.9.lengths_hbm), custom_call_target="tpu_custom_call" | custom-call | tf_op jit(solution)/shard_map/pallas_call | solution.py:211
  34.2 1.2 %slice_bitcast_fusion = (f32[1,8]{1,0:T(1,128)}, f32[1,8]{1,0:T(1,128)}) fusion(f32[2,1,8]{2,1,0:T(1,128)} %shard_map.86), kind=kLoop, calls=%fused_computation | loop fusion | bytes 128 | tf_op jit(solution)/shard_map/squeeze | solution.py:242

commit v4 on v3

--- a/solution.py
+++ b/solution.py
@@ -14,9 +14,9 @@
 
 
 def fused_kernel(
-    heads_hbm, weight_hbm, residual_hbm, gain_ref, head_hbm, targets_hbm, lengths_hbm,
+    heads_hbm, weight_hbm, residual_hbm, gain_hbm, head_hbm, targets_hbm, lengths_hbm,
     out_ref,
-    heads_ref, residual_ref, targets_ref, lengths_ref, weight, head, part, part_in, square_out, square_in, rows, stat_out, stat_in,
+    heads_ref, residual_ref, gain_ref, targets_ref, lengths_ref, weight, head, part, part_in, square_out, square_in, rows, stat_out, stat_in,
     input_sem, weight_sem, head_sem, part_send, part_recv, square_send, square_recv,
     z_send, z_recv, x_send, x_recv, near_send, near_recv, far_send, far_recv,
     stat_send, stat_recv,
@@ -45,20 +45,22 @@
         copy.start()
         return copy
 
+    barrier = pltpu.get_barrier_semaphore()
+    for peer in PEERS:
+        pl.semaphore_signal(barrier, inc=1, device_id=device(*peer), device_id_type=MESH)
     heads_copy = pltpu.make_async_copy(heads_hbm, heads_ref, input_sem.at[0])
     heads_copy.start()
     weight_copy = pltpu.make_async_copy(weight_hbm, weight, weight_sem)
     weight_copy.start()
     residual_copy = pltpu.make_async_copy(residual_hbm, residual_ref, input_sem.at[1])
     residual_copy.start()
+    gain_copy = pltpu.make_async_copy(gain_hbm, gain_ref, input_sem.at[4])
+    gain_copy.start()
     targets_copy = pltpu.make_async_copy(targets_hbm, targets_ref, input_sem.at[2])
     targets_copy.start()
     lengths_copy = pltpu.make_async_copy(lengths_hbm, lengths_ref, input_sem.at[3])
     lengths_copy.start()
     head_copy = pltpu.make_async_copy(head_hbm, head, head_sem)
-    barrier = pltpu.get_barrier_semaphore()
-    for peer in PEERS:
-        pl.semaphore_signal(barrier, inc=1, device_id=device(*peer), device_id_type=MESH)
 
     heads_copy.wait()
     weight_copy.wait()
@@ -82,6 +84,7 @@
     own_square = jnp.sum(hidden * hidden, axis=1, keepdims=True)
     square_out[...] = jnp.broadcast_to(own_square, square_out.shape)
     square_copy = send(square_out, square_in, square_send, square_recv, device(0, 1, 0))
+    gain_copy.wait()
     scaled_gain = gain_ref[...].astype(jnp.float32).reshape(1, depth)
     square_copy.wait_recv()
     sent.append(square_copy)
@@ -211,11 +214,12 @@
     both = pl.pallas_call(
         fused_kernel,
         out_shape=jax.ShapeDtypeStruct((2, 1, shard), f32),
-        in_specs=[hbm, hbm, hbm, vmem, hbm, hbm, hbm],
+        in_specs=[hbm] * 7,
         out_specs=vmem,
         scratch_shapes=[
             pltpu.VMEM(heads_out.shape, bf16),
             pltpu.VMEM(residual.shape, bf16),
+            pltpu.VMEM(norm_gain.shape, bf16),
             pltpu.VMEM(targets.shape, jnp.int32),
             pltpu.SMEM(lengths.shape, jnp.int32),
             pltpu.VMEM((features, depth), bf16),
@@ -227,7 +231,7 @@
             pltpu.VMEM((VOCAB, SEQ, TENSOR, 2 * shard, depth // 2), bf16),
             pltpu.VMEM((SEQ, TENSOR, shard, 128), f32),
             pltpu.VMEM((len(PEERS) + 1, shard, 128), f32),
-            dma((4,)), dma, dma, dma((hops,)), dma((hops,)), dma, dma,
+            dma((5,)), dma, dma, dma((hops,)), dma((hops,)), dma, dma,
             dma((hops,)), dma((hops,)), dma((TENSOR,)), dma((TENSOR,)),
             dma, dma, dma, dma,
             dma((len(PEERS),)), dma((len(PEERS),)),

time: 35.7 us -> 35.1 us (0.983)
  Pallas kernels: 32.9 us -> 32.4 us
    pallas_call x1, Pallas kernels: 32.9 us -> 32.4 us  [fused(): pl.pallas_call(fused_kernel, out_shape=jax.ShapeDtypeStruct((2, 1, shard)...]
where the time goes in v4:
time: 35.1 us; the launch traced here: 34.8 us
  Pallas kernels  32.4 us (92%)
  between operations  1.29 us (4%)
  local copies, waits for them, and re-layouts  1.18 us (3%)
    pallas_call x1, Pallas kernels, fused(): pl.pallas_call(fused_kernel, out_shape=jax.ShapeDtypeStruct((2, 1, shard)...  32.4 us
    squeeze x1, local copies, waits for them, and re-layouts, fused(): return (both[0], both[1])  1.18 us

profile of v4, /device:TPU:0, one launch (start us, length us, event | category | flops | bytes accessed | tf_op | source)
XLA Modules:
  0.0 34.8 jit_solution(11242837894292131392)
XLA Ops:
  1.3 32.4 %shard_map.86 = f32[2,1,8]{2,1,0:T(1,128)} custom-call(bf16[1,32,256]{2,1,0:T(8,128)(2,1)} %heads_hbm.1, bf16[256,2560]{1,0:T(8,128)(2,1)} %weight_hbm.1, bf16[1,8,2560]{2,1,0:T(8,128)(2,1)} %residual_hbm.1, bf16[2560]{0:T(1024)(128)(2,1)} %gain_hbm.1, bf16[384,5120]{1,0:T(8,128)(2,1)} %head_hbm.1, s32[2,32]{1,0:T(2,128)} %targets_hbm.1, s32[1]{0:T(128)S(6)} %copy.9.lengths_hbm), custom_call_target="tpu_custom_call" | custom-call | tf_op jit(solution)/shard_map/pallas_call | solution.py:214
  33.6 1.2 %slice_bitcast_fusion = (f32[1,8]{1,0:T(1,128)}, f32[1,8]{1,0:T(1,128)}) fusion(f32[2,1,8]{2,1,0:T(1,128)} %shard_map.86), kind=kLoop, calls=%fused_computation | loop fusion | bytes 128 | tf_op jit(solution)/shard_map/squeeze | solution.py:246
